TPU v7x, 32 devices: a whole 2x2x4 slice. The times are simulated.
32 devices in a mesh: obs: 4 (over y, x), cell: 8 (over z, core).
Axes of the slice: x: 2, y: 2, z: 4, core: 2. Of those that a mesh axis runs over, the one named last changes fastest.
Arguments:
- log_k: bfloat16 [1572864, 128], P(('obs', 'cell')), may hold values from -6 to 6
- heads_pred: bfloat16 [16384, 128], P(('obs', 'cell')), may hold values from -6 to 6
- slot_well: int32 [16384], P(('obs', 'cell')), may hold values from 0 to 4095, as said below
- tile_count: int32 [32], P(('obs', 'cell')), may hold values from 16 to 512, as said below
- obs_values: float32 [4096, 128], P(('obs', 'cell')), may hold values from -9 to 9
- obs_std: float32 [4096], P(('obs', 'cell')), may hold values from 0.5 to 2
- loc_blocks: int32 [8, 8], replicated, may hold values from 0 to 31, all different within a row
- taper: float32 [8, 8], replicated, may hold values from 0.3 to 1
- lambdas: float32 [4], replicated, may hold values from 0.1 to 10
Outputs:
- posterior: bfloat16 [1572864, 128], P(('obs', 'cell'))
- change_norms: float32 [32, 4, 128], P(('obs', 'cell'))
Inputs may be any that keep to these rules, and one draw needn't show every extreme that they name: `slot_well`: slots below a cell block's count hold the wells lying in that block in increasing order; every well lies in exactly one cell block; other slots hold 0. No cell block holds more than 16 wells of one observation block, and some pairs hold exactly 16. `tile_count`: some cell blocks hold exactly 512 wells. `loc_blocks`: each row names 8 different blocks, and every block is named by some tile.
All inputs are finite; a program needn't handle non-finite values.
Results may differ from a plain program's by a relative error of at most 0.0095.
Values may be sent and summed in bfloat16 or wider, within the bound.
A program may use at most 256 MiB of HBM per device.

v0:
```python
import jax
import jax.numpy as jnp
from jax import lax
from jax.sharding import PartitionSpec as P

CAP = 16


def solve_lambdas(curvature, right_side, lambda_values):
    member_count = curvature.shape[0]
    identity = jnp.eye(member_count, dtype=jnp.float32)
    shifts = (1.0 + lambda_values) * (member_count - 1)
    systems = curvature[None] + shifts[:, None, None] * identity[None]
    factor = jnp.linalg.cholesky(systems)
    targets = jnp.broadcast_to(right_side[None], systems.shape)
    return jax.scipy.linalg.cho_solve((factor, True), targets).astype(jnp.bfloat16)


def on_device(
    log_k, heads_pred, slot_well, tile_count, obs_values, obs_std, loc_blocks, taper, lambdas
):
    n_obs = lax.axis_size("obs")
    n_cell = lax.axis_size("cell")
    device_total = n_obs * n_cell
    slot_total = slot_well.shape[0]
    member_count = heads_pred.shape[1]
    wells_dev = obs_values.shape[0]
    capacity = CAP
    positions = jnp.arange(slot_total, dtype=jnp.int32)
    is_valid = positions < tile_count[0]
    owner_block = slot_well // wells_dev
    owner_row = slot_well % wells_dev
    earlier = jnp.sum(
        (is_valid[None, :] & (owner_block[None, :] < owner_block[:, None])).astype(jnp.int32),
        axis=1,
    )
    slot_rank = positions - earlier
    send_index = jnp.where(is_valid, owner_block * capacity + slot_rank, device_total * capacity)
    send_heads = (
        jnp.zeros((device_total * capacity, member_count), jnp.bfloat16)
        .at[send_index]
        .set(heads_pred, mode="drop")
    )
    send_place = (
        jnp.full((device_total * capacity,), wells_dev, jnp.int32)
        .at[send_index]
        .set(owner_row, mode="drop")
    )
    recv_heads, recv_place = (
        lax.all_to_all(
            send_heads.reshape(device_total, capacity, member_count),
            ("obs", "cell"),
            split_axis=0,
            concat_axis=0,
            tiled=True,
        ),
        lax.all_to_all(
            send_place.reshape(device_total, capacity),
            ("obs", "cell"),
            split_axis=0,
            concat_axis=0,
            tiled=True,
        ),
    )
    predicted = (
        jnp.zeros((wells_dev, member_count), jnp.float32)
        .at[recv_place.reshape(-1)]
        .set(recv_heads.reshape(-1, member_count).astype(jnp.float32), mode="drop")
    )
    member_mean = jnp.mean(predicted, axis=1, keepdims=True)
    scaled = (predicted - member_mean) / obs_std[:, None]
    innovation = (obs_values - predicted) / obs_std[:, None]
    joined = jnp.concatenate([scaled, innovation], axis=1)
    block_gram = jnp.dot(
        scaled.T, joined, precision=lax.Precision.HIGHEST, preferred_element_type=jnp.float32
    )
    cell_place = lax.axis_index("cell")
    tile_range = jnp.arange(n_cell, dtype=jnp.int32)
    band_rows = member_count // n_obs
    banded = lax.all_to_all(
        block_gram.reshape(n_obs, band_rows, 2 * member_count),
        "obs",
        split_axis=0,
        concat_axis=0,
        tiled=True,
    )
    column_blocks = jnp.arange(n_obs, dtype=jnp.int32) * n_cell + cell_place
    column_weight = jnp.sum(
        taper[:, :, None]
        * (loc_blocks[:, :, None] == column_blocks[None, None, :]).astype(jnp.float32),
        axis=1,
    )
    dest_index = jnp.arange(band_rows * lax.axis_size("cell") // band_rows, dtype=jnp.int32)
    selector = (dest_index[:, None] == tile_range[None, :]).astype(jnp.float32)
    weight_rows = jnp.sum(selector[:, :, None] * column_weight[None, :, :], axis=1)
    terms = jnp.sum(weight_rows[:, :, None, None] * banded[None], axis=1)
    band_part = lax.psum_scatter(
        terms.reshape(band_rows * lax.axis_size("cell"), 2 * member_count),
        "cell",
        scatter_dimension=0,
        tiled=True,
    )
    tile_gram = lax.all_gather(band_part, "obs", axis=0, tiled=True)
    curvature = tile_gram[:, :member_count]
    right_side = tile_gram[:, member_count:]
    lambda_total = lambdas.shape[0]
    transforms = solve_lambdas(curvature, right_side, lambdas)
    field = log_k.astype(jnp.float32)
    anomalies = (field - jnp.mean(field, axis=1, keepdims=True)).astype(jnp.bfloat16)
    joined_transforms = jnp.transpose(transforms, (1, 0, 2)).reshape(
        member_count, lambda_total * member_count
    )
    change = jnp.dot(anomalies, joined_transforms, preferred_element_type=jnp.float32)
    change = change.reshape(field.shape[0], lambda_total, member_count)
    updated = (field + change[:, 0, :]).astype(jnp.bfloat16)
    change_norms = jnp.sum(change * change, axis=0)
    return (updated, change_norms[None])


def solution(mesh):
    return jax.shard_map(
        on_device,
        mesh=mesh,
        in_specs=(
            P(("obs", "cell"), None),
            P(("obs", "cell"), None),
            P(("obs", "cell")),
            P(("obs", "cell")),
            P(("obs", "cell"), None),
            P(("obs", "cell")),
            P(),
            P(),
            P(),
        ),
        out_specs=(P(("obs", "cell"), None), P(("obs", "cell"), None, None)),
        check_vma=False,
    )
```

profile of v0, /device:TPU:0, one launch (start us, length us, event | category | flops | bytes accessed | tf_op | source)
XLA Modules:
  0.0 246.8 jit_solution(12959958154770944948)
XLA Ops:
  7.8 0.7 add_select_fusion
  8.8 2.4 scatter_custom_fusion
  11.3 0.7 all_to_all.12
  11.9 7.3 %all-to-all-start = ((s32[32,1,16]{2,1,0:T(1,128)}), s32[32,1,16]{2,1,0:T(1,128)S(1)}, u32[]{:S(2)}, u32[]{:S(2)}) async-start(s32[32,1,16]{2,1,0:T(1,128)} %bitcast.2), calls=%async_computation | async-start | bytes 32768 | tf_op jit(solution)/shard_map/all_to_all | solution.py:57
  19.3 7.6 %convert_reduce_fusion = f32[49152]{0:T(1024)S(1)} fusion(bf16[49152,128]{1,0:T(8,128)(2,1)} %param.9), kind=kLoop, calls=%fused_computation.6 | loop fusion | flops 12533760 | bytes 12779520 | tf_op jit(solution)/shard_map/reduce_sum | solution.py:109
  26.9 0.9 select_reduce_fusion.1
  27.8 2.7 %scatter_custom_fusion.1 = bf16[512,128]{1,0:T(8,128)(2,1)} fusion(s32[512]{0:T(512)S(1)} %compare_select_fusion.1, bf16[512,128]{1,0:T(8,128)(2,1)} %param.10, bf16[]{:T(256)} %constant.101.clone.1), kind=kCustom, calls=%fused_computation.34 | custom fusion | bytes 131584 | tf_op jit(solution)/shard_map/scatter | solution.py:42
  30.5 5.8 %all-to-all-start.1 = ((bf16[32,16,128]{2,1,0:T(8,128)(2,1)}), bf16[32,16,128]{2,1,0:T(8,128)(2,1)S(1)}, u32[]{:S(2)}, u32[]{:S(2)}) async-start(bf16[32,16,128]{2,1,0:T(8,128)(2,1)} %bitcast.4), calls=%async_computation.1 | async-start | bytes 262144 | tf_op jit(solution)/shard_map/all_to_all | solution.py:50
  36.8 0.7 reduce.9
  37.6 6.9 %all-to-all-done.1 = bf16[32,16,128]{2,1,0:T(8,128)(2,1)S(1)} async-done(((bf16[32,16,128]{2,1,0:T(8,128)(2,1)}), bf16[32,16,128]{2,1,0:T(8,128)(2,1)S(1)}, u32[]{:S(2)}, u32[]{:S(2)}) %all-to-all-start.1) | async-done | bytes 131104 | tf_op jit(solution)/shard_map/all_to_all | solution.py:50
  44.5 1.7 scatter_custom_fusion.2
  46.4 0.9 subtract_divide_fusion
  47.3 1.0 fusion.12
  48.3 3.3 %all-to-all-start.2 = ((f32[4,32,256]{2,1,0:T(8,128)}), f32[4,32,256]{2,1,0:T(8,128)S(1)}, u32[]{:S(2)}, u32[]{:S(2)}) async-start(f32[4,32,256]{2,1,0:T(8,128)} %bitcast.6), calls=%async_computation.2 | async-start | bytes 262144 | tf_op jit(solution)/shard_map/all_to_all | solution.py:80
  51.8 4.8 %all-to-all-done.2 = f32[4,32,256]{2,1,0:T(8,128)S(1)} async-done(((f32[4,32,256]{2,1,0:T(8,128)}), f32[4,32,256]{2,1,0:T(8,128)S(1)}, u32[]{:S(2)}, u32[]{:S(2)}) %all-to-all-start.2) | async-done | bytes 131104 | tf_op jit(solution)/shard_map/all_to_all | solution.py:80
  56.6 0.8 multiply_reduce_fusion.1
  57.6 0.7 add_multiply_fusion.1
  58.2 26.9 %reduce-scatter.2.cloned.1.call-done = f32[32,256]{1,0:T(8,128)} async-done(((f32[256,256]{1,0:T(8,128)}), f32[32,256]{1,0:T(8,128)}) %reduce-scatter.2.cloned.1.call-update) | async-done | bytes 32784 | tf_op jit(solution)/shard_map/reduce_scatter | solution.py:97
  85.2 8.8 %all_gather.3 = f32[128,256]{1,0:T(8,128)S(1)} all-gather(f32[32,256]{1,0:T(8,128)} %reduce-scatter.2.cloned.1.call-done), channel_id=1, replica_groups=mesh['obs'=4,'cell'=8] {'obs'}, dimensions={0}, use_global_device_ids=true | all-gather | bytes 163840 | tf_op jit(solution)/shard_map/all_gather | solution.py:103
  94.2 46.9 %custom-call.11 = f32[4,128,128]{2,1,0:T(8,128)S(1)} custom-call(f32[4,128,128]{2,1,0:T(8,128)S(1)} %add_multiply_fusion), custom_call_target="Cholesky" | custom-call | tf_op jit(solution)/shard_map/jit(cholesky)/cholesky | solution.py:14
  141.4 39.3 %custom-call.12 = f32[4,1,128,128]{2,3,1,0:T(8,128)S(1)} custom-call(f32[4,1,128,128]{3,2,1,0:T(8,128)S(1)} %select_bitcast_fusion), custom_call_target="InvertDiagBlocksLowerTriangular" | custom-call | tf_op jit(solution)/shard_map/jit(_cho_solve)/vmap()/triangular_solve | solution.py:16
  181.3 0.7 fusion.6
  182.0 40.6 %multiply_reduce_fusion = (f32[4,128]{1,0:T(4,128)}, f32[49152,4,128]{2,0,1:T(8,128)}) fusion(bf16[4,128,128]{2,1,0:T(8,128)(2,1)S(1)} %fusion.6, bf16[49152,128]{1,0:T(8,128)(2,1)} %param.9, f32[49152]{0:T(1024)S(1)} %broadcast_multiply_fusion), kind=kOutput, calls=%fused_computation.3 | convolution fusion | flops 6511656448 | bytes 113575936 | tf_op jit(solution)/shard_map/dot_general | solution.py:113
  222.6 17.4 %fusion.1 = bf16[49152,128]{1,0:T(8,128)(2,1)} fusion(bf16[49152,128]{1,0:T(8,128)(2,1)} %param.9, f32[49152,4,128]{2,0,1:T(8,128)} %get-tuple-element.10), kind=kLoop, calls=%fused_computation.8 | loop fusion | flops 18874368 | bytes 50331648 | tf_op jit(solution)/shard_map/convert_element_type | solution.py:115
  (26 shorter events, 2.4 us)
Async XLA Ops:
  11.9 18.5 %all-to-all-start = ((s32[32,1,16]{2,1,0:T(1,128)}), s32[32,1,16]{2,1,0:T(1,128)S(1)}, u32[]{:S(2)}, u32[]{:S(2)}) async-start(s32[32,1,16]{2,1,0:T(1,128)} %bitcast.2), calls=%async_computation | async-start | bytes 32768 | tf_op jit(solution)/shard_map/all_to_all | solution.py:57
  30.5 14.0 %all-to-all-start.1 = ((bf16[32,16,128]{2,1,0:T(8,128)(2,1)}), bf16[32,16,128]{2,1,0:T(8,128)(2,1)S(1)}, u32[]{:S(2)}, u32[]{:S(2)}) async-start(bf16[32,16,128]{2,1,0:T(8,128)(2,1)} %bitcast.4), calls=%async_computation.1 | async-start | bytes 262144 | tf_op jit(solution)/shard_map/all_to_all | solution.py:50
  48.3 8.4 %all-to-all-start.2 = ((f32[4,32,256]{2,1,0:T(8,128)}), f32[4,32,256]{2,1,0:T(8,128)S(1)}, u32[]{:S(2)}, u32[]{:S(2)}) async-start(f32[4,32,256]{2,1,0:T(8,128)} %bitcast.6), calls=%async_computation.2 | async-start | bytes 262144 | tf_op jit(solution)/shard_map/all_to_all | solution.py:80
  51.6 33.6 %reduce-scatter.2.cloned.1.call-start = ((), (), s32[]{:S(2)}) async-start(), calls=%async_computation.4 | async-start | bytes 294912 | tf_op jit(solution)/shard_map/reduce_scatter | solution.py:97
Sparse Core Ops, SparseCore 0:
  57.6 27.4 reduce-scatter.1
where the time goes:
time: 247 us
  other arithmetic  119 us (48%)
  matrix products  42.8 us (17%)
  waiting for transfers between devices  38.6 us (16%)
  starting transfers between devices  16.5 us (7%)
  between operations  14.9 us (6%)
  blocking collectives  8.81 us (4%)
  local copies, waits for them, and re-layouts  6.59 us (3%)
    another operation x4, other arithmetic, solve_lambdas(): factor = jnp.linalg.cholesky(systems)  47.1 us
    dot_general x1, matrix products, on_device(): jnp.dot(anomalies, joined_transforms, preferred_element_type=jnp.float32)  40.6 us
    another operation x3, other arithmetic, solve_lambdas(): jax.scipy.linalg.cho_solve((factor, True), targets).astype(jnp.bfloat16)  39.4 us
    reduce_scatter x1, waiting for transfers between devices, on_device(): lax.psum_scatter(terms.reshape(band_rows * lax.axis_size('cell'), 2 * mem...  26.9 us
    convert_element_type x1, other arithmetic, on_device(): updated = (field + change[:, 0, :]).astype(jnp.bfloat16)  17.4 us
    all_gather x1, blocking collectives, on_device(): tile_gram = lax.all_gather(band_part, 'obs', axis=0, tiled=True)  8.81 us
    reduce_sum x1, other arithmetic, on_device(): jnp.mean(field, axis=1, keepdims=True)  7.62 us
    all_to_all x1, starting transfers between devices, on_device(): lax.all_to_all(send_place.reshape(device_total, capacity), ('obs', 'cell'...  7.3 us
  transfers between devices with their start and end apart: 4, of which 3 were waited for; matrix products, arithmetic and copies ran while one was open for 5% of the time, Pallas kernels for 0%

commit v1 on v0

v1 whole, which is shorter than its diff:
```python
import functools

import jax
import jax.numpy as jnp
from jax import lax
from jax.experimental import pallas as pl
from jax.experimental.pallas import tpu as pltpu
from jax.sharding import PartitionSpec as P

CAP = 16
PIECES = 4
MESH = pl.DeviceIdType.MESH
HIGHEST = lax.Precision.HIGHEST
F32 = jnp.float32
BF16 = jnp.bfloat16


def dot(a, b, precision=None):
    return jnp.dot(a, b, precision=precision, preferred_element_type=F32)


def dot_rows(a, b, precision=None):
    return lax.dot_general(
        a, b, (((0,), (0,)), ((), ())), precision=precision, preferred_element_type=F32
    )


def divide(x, n):
    if n & (n - 1) == 0:
        return lax.shift_right_logical(x, jnp.full(x.shape, n.bit_length() - 1, x.dtype))
    return x // n


def rows_per_step(total, most):
    step = most
    while total % step:
        step //= 2
    return step


def gram_kernel(
    n_obs, n_cell, loc,
    heads_ref, well_ref, count_ref, obs_ref, std_ref, loc_ref, taper_ref, log_k_ref,
    gram_ref, cov_ref,
    field, send_heads, recv_heads, send_idx, recv_idx, obs_send, obs_all, pred_send, pred_all,
    s_all, d_all, part, bands, band_sum, summed, field_sem, send_sem, recv_sem,
):
    total = n_obs * n_cell
    o, c = lax.axis_index("obs"), lax.axis_index("cell")
    me = o * n_cell + c
    cells, members = field.shape
    wells = obs_ref.shape[0]
    slots = heads_ref.shape[0]
    piece_rows = cells // PIECES

    def piece_copy(p):
        rows = pl.ds(p * piece_rows, piece_rows)
        return pltpu.make_async_copy(log_k_ref.at[rows], field.at[rows], field_sem.at[p])

    for p in range(PIECES):
        piece_copy(p).start()

    barrier = pltpu.get_barrier_semaphore()

    @pl.loop(1, total)
    def _(i):
        to = lax.rem(me + i, total)
        pl.semaphore_signal(
            barrier, inc=1, device_id=(to // n_cell, lax.rem(to, n_cell)), device_id_type=MESH
        )

    well = well_ref[...]
    lane = lax.broadcasted_iota(jnp.int32, (1, slots), 1)
    owner = divide(well, wells)
    place_in = (well - owner * wells + 1).astype(F32)
    owner = jnp.where(lane < count_ref[0], owner, total)
    lane_f = lane.astype(F32)
    group = 8
    rows_now = group * CAP
    row_at = lax.broadcasted_iota(jnp.int32, (rows_now, 1), 0)
    in_group = divide(row_at, CAP)
    rank = (row_at - in_group * CAP).astype(F32)
    well_lane = lax.broadcasted_iota(jnp.int32, (1, wells), 1).astype(F32)

    @pl.loop(0, total // group)
    def _(i):
        dest = in_group + i * group
        start = jnp.sum(jnp.where(owner < dest, 1.0, 0.0), axis=1, keepdims=True)
        hit = jnp.where((owner == dest) & (lane_f == start + rank), 1.0, 0.0)
        rows = pl.ds(pl.multiple_of(i * rows_now, rows_now), rows_now)
        send_heads[rows, :] = dot(hit.astype(BF16), heads_ref[...]).astype(BF16)
        place = jnp.sum(hit * place_in, axis=1, keepdims=True) - 1.0
        ranks = jnp.where(place == well_lane, rank + 1.0, 0.0)
        for q in range(group):
            send_idx[i * group + q] = (
                jnp.sum(ranks[q * CAP : (q + 1) * CAP], axis=0, keepdims=True) - 1.0
            )

    obs_send[:wells, :] = obs_ref[...]
    obs_send[wells:, :] = jnp.broadcast_to(std_ref[...], (8, wells))
    pl.semaphore_wait(barrier, total - 1)

    def head_rows(d):
        return pl.ds(pl.multiple_of(d * CAP, CAP), CAP)

    @pl.loop(1, total)
    def _(i):
        to = lax.rem(me + i, total)
        device = (to // n_cell, lax.rem(to, n_cell))
        pltpu.make_async_remote_copy(
            src_ref=send_heads.at[head_rows(to)], dst_ref=recv_heads.at[head_rows(me)],
            send_sem=send_sem.at[0], recv_sem=recv_sem.at[0],
            device_id=device, device_id_type=MESH,
        ).start()
        pltpu.make_async_remote_copy(
            src_ref=send_idx.at[to], dst_ref=recv_idx.at[me],
            send_sem=send_sem.at[1], recv_sem=recv_sem.at[1],
            device_id=device, device_id_type=MESH,
        ).start()

    pltpu.make_async_copy(
        send_heads.at[head_rows(me)], recv_heads.at[head_rows(me)], recv_sem.at[0]
    ).start()
    pltpu.make_async_copy(send_idx.at[me], recv_idx.at[me], recv_sem.at[1]).start()

    def to_cells(src, dst, at):
        @pl.loop(1, n_cell)
        def _(i):
            pltpu.make_async_remote_copy(
                src_ref=src, dst_ref=dst.at[c], send_sem=send_sem.at[at],
                recv_sem=recv_sem.at[at],
                device_id=(o, lax.rem(c + i, n_cell)), device_id_type=MESH,
            ).start()

        pltpu.make_async_copy(src, dst.at[c], recv_sem.at[at]).start()

    to_cells(obs_send, obs_all, 2)

    ones = jnp.ones((members, members), BF16)
    step_rows = rows_per_step(piece_rows, 1024)
    cov_ref[...] = jnp.zeros_like(cov_ref)

    def covariance(p):
        piece_copy(p).wait()

        @pl.loop(0, piece_rows // step_rows)
        def _(i):
            at = pl.multiple_of(p * piece_rows + i * step_rows, step_rows)
            x = field[pl.ds(at, step_rows), :]
            mean = dot(x, ones) * (1.0 / members)
            anomalies = (x.astype(F32) - mean).astype(BF16)
            cov_ref[...] += dot_rows(anomalies, anomalies)

    def arrived(ref, at):
        pltpu.make_async_copy(ref, ref, recv_sem.at[at]).wait()

    covariance(0)
    arrived(recv_heads, 0)
    arrived(recv_idx, 1)
    ranks_at = lax.broadcasted_iota(jnp.int32, (total, CAP, wells), 1).astype(F32)
    take = jnp.where(recv_idx[...] == ranks_at, 1.0, 0.0).reshape(total * CAP, wells)
    pred_send[...] = dot_rows(take.astype(BF16), recv_heads[...]).astype(BF16)
    to_cells(pred_send, pred_all, 3)

    covariance(1)
    covariance(2)
    arrived(obs_all, 2)
    arrived(pred_all, 3)
    eye = (
        lax.broadcasted_iota(jnp.int32, (wells, wells), 0)
        == lax.broadcasted_iota(jnp.int32, (wells, wells), 1)
    )

    @pl.loop(0, n_cell)
    def _(b):
        block = o * n_cell + b
        weight = jnp.float32(0.0)
        for k in range(loc):
            weight = weight + jnp.where(loc_ref[c, k] == block, taper_ref[c, k], 0.0)
        std = jnp.sum(
            jnp.where(eye, obs_all[b, pl.ds(wells, 1), :], 0.0), axis=1, keepdims=True
        )
        inverse = 1.0 / std
        pred = pred_all[b].astype(F32)
        mean = jnp.mean(pred, axis=1, keepdims=True)
        scaled = (pred - mean) * inverse
        rows = pl.ds(pl.multiple_of(b * wells, wells), wells)
        s_all[rows, :] = scaled * weight
        d_all[rows, :members] = scaled
        d_all[rows, members:] = (obs_all[b, pl.ds(0, wells), :] - pred) * inverse

    product = dot_rows(s_all[...], d_all[...], HIGHEST)
    band = members // n_obs
    part[...] = product.reshape(part.shape)

    def obs_copies(src_of, dst, at):
        @pl.loop(1, n_obs)
        def _(i):
            to = lax.rem(o + i, n_obs)
            pltpu.make_async_remote_copy(
                src_ref=src_of(to), dst_ref=dst.at[o], send_sem=send_sem.at[at],
                recv_sem=recv_sem.at[at], device_id=(to, c), device_id_type=MESH,
            ).start()

        pltpu.make_async_copy(src_of(o), dst.at[o], recv_sem.at[at]).start()

    obs_copies(lambda to: part.at[to], bands, 4)
    arrived(bands, 4)
    band_sum[...] = jnp.sum(bands[...], axis=0)
    obs_copies(lambda to: band_sum, summed, 5)
    covariance(3)
    arrived(summed, 5)
    gram_ref[...] = summed[...].reshape(gram_ref.shape)

    def sent(ref, at):
        pltpu.make_async_copy(ref, ref, send_sem.at[at]).wait()

    sent(recv_heads.at[pl.ds(0, (total - 1) * CAP)], 0)
    sent(recv_idx.at[pl.ds(0, total - 1)], 1)
    sent(obs_all.at[pl.ds(0, n_cell - 1)], 2)
    sent(pred_all.at[pl.ds(0, n_cell - 1)], 3)
    sent(bands.at[pl.ds(0, n_obs - 1)], 4)
    sent(summed.at[pl.ds(0, n_obs - 1)], 5)


def update_kernel(
    gram_ref, cov_ref, lambda_ref, log_k_ref, posterior_ref, norms_ref,
    field, inverse, weights, in_sem, out_sem,
):
    cells, members = field.shape
    groups = in_sem.shape[0]
    group_rows = cells // groups
    lambda_total = lambda_ref.shape[0]

    def group_copy(g, back):
        rows = pl.ds(g * group_rows, group_rows)
        if back:
            return pltpu.make_async_copy(field.at[rows], posterior_ref.at[rows], out_sem.at[g])
        return pltpu.make_async_copy(log_k_ref.at[rows], field.at[rows], in_sem.at[g])

    for g in range(groups):
        group_copy(g, False).start()

    curvature = gram_ref[:, :members]
    top = jnp.max(jnp.sum(jnp.abs(curvature), axis=1, keepdims=True))
    eye = jnp.where(
        lax.broadcasted_iota(jnp.int32, (members, members), 0)
        == lax.broadcasted_iota(jnp.int32, (members, members), 1),
        1.0, 0.0,
    )
    shifts = [(1.0 + lambda_ref[l]) * (members - 1) for l in range(lambda_total)]

    def system(l):
        return gram_ref[:, :members] + shifts[l] * eye

    rhos = []
    for l in range(lambda_total):
        first = 2.0 / (2.0 * shifts[l] + top)
        rho = top * (0.5 * first)
        gain = 2.0 / (2.0 - rho * rho)
        inverse[l] = (gain * first) * (2.0 * eye - first * system(l))
        rhos.append(rho * rho / (2.0 - rho * rho))

    def largest(values):
        return functools.reduce(jnp.maximum, values)

    def step(carry):
        count, rhos = carry
        after = []
        halves = [dot(system(l), inverse[l], HIGHEST) for l in range(lambda_total)]
        for l in range(lambda_total):
            rho = rhos[l]
            gain = 2.0 / (2.0 - rho * rho)
            x = inverse[l]
            inverse[l] = gain * (2.0 * x - dot(x, halves[l], HIGHEST))
            after.append(rho * rho / (2.0 - rho * rho))
        return count + 1, tuple(after)

    lax.while_loop(
        lambda carry: (largest(carry[1]) > 2e-3) & (carry[0] < 40),
        step,
        (jnp.int32(0), tuple(rhos)),
    )

    right = gram_ref[:, members:]
    firsts = [dot(inverse[l], right, HIGHEST) for l in range(lambda_total)]
    misses = [right - dot(system(l), firsts[l], HIGHEST) for l in range(lambda_total)]
    for l in range(lambda_total):
        solved = firsts[l] + dot(inverse[l], misses[l], HIGHEST)
        transform = solved.astype(BF16).astype(F32)
        if l == 0:
            centred = transform - jnp.mean(transform, axis=0, keepdims=True) + eye
            high = centred.astype(BF16)
            weights[:members, :] = high
            weights[members:, :] = (centred - high.astype(F32)).astype(BF16)
        spread = dot(cov_ref[...], transform, HIGHEST)
        norms_ref[pl.ds(l, 1), :] = jnp.sum(transform * spread, axis=0, keepdims=True)

    step_rows = rows_per_step(group_rows, 1024)
    for g in range(groups):
        group_copy(g, False).wait()

        @pl.loop(0, group_rows // step_rows)
        def _(i):
            rows = pl.ds(pl.multiple_of(g * group_rows + i * step_rows, step_rows), step_rows)
            x = field[rows, :]
            field[rows, :] = dot(jnp.concatenate([x, x], axis=1), weights[...]).astype(BF16)

        group_copy(g, True).start()
    for g in range(groups):
        group_copy(g, True).wait()


def on_device(
    log_k, heads_pred, slot_well, tile_count, obs_values, obs_std, loc_blocks, taper, lambdas
):
    n_obs = lax.axis_size("obs")
    n_cell = lax.axis_size("cell")
    total = n_obs * n_cell
    cells, members = log_k.shape
    slots = slot_well.shape[0]
    wells = obs_values.shape[0]
    band = members // n_obs
    vmem = pl.BlockSpec(memory_space=pltpu.VMEM)
    smem = pl.BlockSpec(memory_space=pltpu.SMEM)
    hbm = pl.BlockSpec(memory_space=pl.ANY)
    gram, cov = pl.pallas_call(
        functools.partial(gram_kernel, n_obs, n_cell, loc_blocks.shape[1]),
        out_shape=(
            jax.ShapeDtypeStruct((members, 2 * members), F32),
            jax.ShapeDtypeStruct((members, members), F32),
        ),
        in_specs=[vmem, vmem, smem, vmem, vmem, smem, smem, hbm],
        out_specs=(vmem, vmem),
        scratch_shapes=[
            pltpu.VMEM((cells, members), BF16),
            pltpu.VMEM((total * CAP, members), BF16),
            pltpu.VMEM((total * CAP, members), BF16),
            pltpu.VMEM((total, 1, wells), F32),
            pltpu.VMEM((total, 1, wells), F32),
            pltpu.VMEM((wells + 8, members), F32),
            pltpu.VMEM((n_cell, wells + 8, members), F32),
            pltpu.VMEM((wells, members), BF16),
            pltpu.VMEM((n_cell, wells, members), BF16),
            pltpu.VMEM((n_cell * wells, members), F32),
            pltpu.VMEM((n_cell * wells, 2 * members), F32),
            pltpu.VMEM((n_obs, band, 2 * members), F32),
            pltpu.VMEM((n_obs, band, 2 * members), F32),
            pltpu.VMEM((band, 2 * members), F32),
            pltpu.VMEM((n_obs, band, 2 * members), F32),
            pltpu.SemaphoreType.DMA((PIECES,)),
            pltpu.SemaphoreType.DMA((6,)),
            pltpu.SemaphoreType.DMA((6,)),
        ],
        compiler_params=pltpu.CompilerParams(
            collective_id=0, has_side_effects=True, vmem_limit_bytes=48 << 20
        ),
        name="gram",
    )(
        heads_pred, slot_well.reshape(1, slots), tile_count, obs_values,
        obs_std.reshape(1, wells), loc_blocks, taper, log_k,
    )
    lambda_total = lambdas.shape[0]
    groups = 12
    posterior, norms = pl.pallas_call(
        update_kernel,
        out_shape=(
            jax.ShapeDtypeStruct((cells, members), BF16),
            jax.ShapeDtypeStruct((lambda_total, members), F32),
        ),
        in_specs=[vmem, vmem, smem, hbm],
        out_specs=(hbm, vmem),
        scratch_shapes=[
            pltpu.VMEM((cells, members), BF16),
            pltpu.VMEM((lambda_total, members, members), F32),
            pltpu.VMEM((2 * members, members), BF16),
            pltpu.SemaphoreType.DMA((groups,)),
            pltpu.SemaphoreType.DMA((groups,)),
        ],
        compiler_params=pltpu.CompilerParams(vmem_limit_bytes=48 << 20),
        name="update",
    )(gram, cov, lambdas, log_k)
    return posterior, norms[None]


def solution(mesh):
    return jax.shard_map(
        on_device,
        mesh=mesh,
        in_specs=(
            P(("obs", "cell"), None),
            P(("obs", "cell"), None),
            P(("obs", "cell")),
            P(("obs", "cell")),
            P(("obs", "cell"), None),
            P(("obs", "cell")),
            P(),
            P(),
            P(),
        ),
        out_specs=(P(("obs", "cell"), None), P(("obs", "cell"), None, None)),
        check_vma=False,
    )
```

time: 247 us -> 68.4 us (0.28)
  other arithmetic: 119 us -> 0 us
  Pallas kernels: 0 us -> 62.3 us
  matrix products: 42.8 us -> 0 us
  waiting for transfers between devices: 38.6 us -> 0 us
  starting transfers between devices: 16.5 us -> 0 us
  between operations: 14.9 us -> 1.33 us
  blocking collectives: 8.81 us -> 0 us
    another operation x7 -> x0, other arithmetic: 86.5 us -> none  [the longest x4 47.1 us: solve_lambdas(): factor = jnp.linalg.cholesky(systems)]
    pallas_call x0 -> x2, Pallas kernels: none -> 62.3 us  [the longest x1 40.9 us: on_device(): pl.pallas_call(functools.partial(gram_kernel, n_obs, n_cell, loc_blocks.s...]
    dot_general x2 -> x0, matrix products: 41.6 us -> none  [the longest x1 40.6 us: on_device(): jnp.dot(anomalies, joined_transforms, preferred_element_type=jnp.float32)]
    reduce_scatter x1 -> x0, waiting for transfers between devices: 26.9 us -> none  [on_device(): lax.psum_scatter(terms.reshape(band_rows * lax.axis_size('cell'), 2 * mem...]
    convert_element_type x3 -> x0, other arithmetic: 17.4 us -> none  [the longest x1 17.4 us: on_device(): updated = (field + change[:, 0, :]).astype(jnp.bfloat16)]
    all_to_all x3 -> x0, starting transfers between devices: 16.5 us -> none  [the longest x1 7.3 us: on_device(): lax.all_to_all(send_place.reshape(device_total, capacity), ('obs', 'cell'...]
    all_to_all x3 -> x0, waiting for transfers between devices: 11.7 us -> none  [the longest x1 6.87 us: on_device(): lax.all_to_all(send_heads.reshape(device_total, capacity, member_count),...]
    reduce_sum x6 -> x0, other arithmetic: 9.8 us -> none  [the longest x1 7.62 us: on_device(): jnp.mean(field, axis=1, keepdims=True)]
  transfers between devices with their start and end apart: 4 -> 0, of which waited for: 3 -> 0; matrix products, arithmetic and copies ran while one was open for 5% -> 0% of each run, Pallas kernels for 0% -> 0%
where the time goes in v1:
time: 68.4 us; the launch traced here: 68.1 us
  Pallas kernels  62.3 us (91%)
  local copies, waits for them, and re-layouts  4.45 us (7%)
  between operations  1.33 us (2%)
    pallas_call x1, Pallas kernels, on_device(): pl.pallas_call(functools.partial(gram_kernel, n_obs, n_cell, loc_blocks.s...  40.9 us
    pallas_call x1, Pallas kernels, on_device(): pl.pallas_call(update_kernel, out_shape=(jax.ShapeDtypeStruct((cells, mem...  21.5 us
    unnamed x14, local copies, waits for them, and re-layouts  4.45 us

profile of v1, /device:TPU:0, one launch (start us, length us, event | category | flops | bytes accessed | tf_op | source)
XLA Modules:
  0.0 68.1 jit_solution(13506260970411334754)
XLA Ops:
  0.6 0.0 copy-start.6
  1.3 0.0 copy-start
  1.3 0.9 %copy-done = bf16[512,128]{1,0:T(8,128)(2,1)S(1)} copy-done((bf16[512,128]{1,0:T(8,128)(2,1)S(1)}, bf16[512,128]{1,0:T(8,128)(2,1)}, u32[]{:S(2)}) %copy-start) | copy-done | bytes 131096
  2.2 0.0 copy-start.1
  2.2 0.8 %copy-done.1 = f32[128,128]{1,0:T(8,128)S(1)} copy-done((f32[128,128]{1,0:T(8,128)S(1)}, f32[128,128]{1,0:T(8,128)}, u32[]{:S(2)}) %copy-start.1) | copy-done | bytes 65560
  3.0 0.0 copy-start.2
  3.0 0.7 %copy-done.2 = s32[8,8]{1,0:T(8,128)S(1)} copy-done((s32[8,8]{1,0:T(8,128)S(1)}, s32[8,8]{1,0:T(8,128)}, u32[]{:S(2)}) %copy-start.2) | copy-done | bytes 280
  3.7 0.0 copy-start.3
  3.7 0.7 %copy-done.3 = f32[8,8]{1,0:T(8,128)S(1)} copy-done((f32[8,8]{1,0:T(8,128)S(1)}, f32[8,8]{1,0:T(8,128)}, u32[]{:S(2)}) %copy-start.3) | copy-done | bytes 280
  4.4 0.0 copy-start.4
  4.4 0.7 copy-done.4
  5.1 0.0 copy-start.5
  5.1 0.7 copy-done.5
  5.8 40.9 %gram.1 = (f32[128,256]{1,0:T(8,128)S(1)}, f32[128,128]{1,0:T(8,128)S(1)}) custom-call(bf16[512,128]{1,0:T(8,128)(2,1)S(1)} %copy-done, s32[1,512]{1,0:T(1,128)S(1)} %bitcast.3, s32[1]{0:T(128)S(6)} %copy.11.count_ref, f32[128,128]{1,0:T(8,128)S(1)} %copy-done.1, f32[1,128]{1,0:T(1,128)S(1)} %bitcast.4, s32[8,8]{1,0:T(8,128)S(1)} %copy-done.2, ...), custom_call_target="tpu_custom_call" | custom-call | tf_op jit(solution)/shard_map/gram/pallas_call | solution.py:327
  46.6 0.0 copy-done.6
  46.6 21.5 %update.1 = (bf16[49152,128]{1,0:T(8,128)(2,1)}, f32[4,128]{1,0:T(4,128)}) custom-call(f32[128,256]{1,0:T(8,128)S(1)} %get-tuple-element.6.gram_ref, f32[128,128]{1,0:T(8,128)S(1)} %get-tuple-element.7.cov_ref, f32[4]{0:T(128)S(1)} %copy-done.6, bf16[49152,128]{1,0:T(8,128)(2,1)} %log_k_ref.3), custom_call_target="tpu_custom_call" | custom-call | tf_op jit(solution)/shard_map/update/pallas_call | solution.py:365
Async XLA Ops:
  0.6 46.0 %copy-start.6 = (f32[4]{0:T(128)S(1)}, f32[4]{0:T(128)}, u32[]{:S(2)}) copy-start(f32[4]{0:T(128)} %lambda_ref.1) | copy-start | bytes 52
  1.3 0.9 %copy-start = (bf16[512,128]{1,0:T(8,128)(2,1)S(1)}, bf16[512,128]{1,0:T(8,128)(2,1)}, u32[]{:S(2)}) copy-start(bf16[512,128]{1,0:T(8,128)(2,1)} %heads_ref.1) | copy-start | bytes 393220
  2.2 0.8 %copy-start.1 = (f32[128,128]{1,0:T(8,128)S(1)}, f32[128,128]{1,0:T(8,128)}, u32[]{:S(2)}) copy-start(f32[128,128]{1,0:T(8,128)} %obs_ref.1) | copy-start | bytes 196612
  3.0 0.7 %copy-start.2 = (s32[8,8]{1,0:T(8,128)S(1)}, s32[8,8]{1,0:T(8,128)}, u32[]{:S(2)}) copy-start(s32[8,8]{1,0:T(8,128)} %loc_ref.1) | copy-start | bytes 772
  3.7 0.7 %copy-start.3 = (f32[8,8]{1,0:T(8,128)S(1)}, f32[8,8]{1,0:T(8,128)}, u32[]{:S(2)}) copy-start(f32[8,8]{1,0:T(8,128)} %taper_ref.1) | copy-start | bytes 772
  4.4 0.7 %copy-start.4 = (s32[512]{0:T(512)S(1)}, s32[512]{0:T(512)}, u32[]{:S(2)}) copy-start(s32[512]{0:T(512)} %param.11) | copy-start | bytes 6148
  5.1 0.7 copy-start.5

commit v2 on v1

--- a/solution.py
+++ b/solution.py
@@ -25,6 +25,27 @@
     )
 
 
+def split(x):
+    high = x.astype(BF16)
+    rest = x - high.astype(F32)
+    middle = rest.astype(BF16)
+    return high, middle, (rest - middle.astype(F32)).astype(BF16)
+
+
+def product(a, b):
+    a_high, a_middle, a_low = split(a)
+    b_high, b_middle, b_low = split(b)
+    pair = jnp.concatenate([b_high, b_middle], axis=1)
+    large = dot(
+        jnp.concatenate([a_high, a_middle], axis=1), jnp.concatenate([pair, pair], axis=0)
+    )
+    small = dot(
+        jnp.concatenate([a_low, a_high], axis=1), jnp.concatenate([b_high, b_low], axis=0)
+    )
+    columns = b.shape[1]
+    return large[:, :columns] + (large[:, columns:] + small)
+
+
 def divide(x, n):
     if n & (n - 1) == 0:
         return lax.shift_right_logical(x, jnp.full(x.shape, n.bit_length() - 1, x.dtype))
@@ -39,17 +60,17 @@
 
 
 def gram_kernel(
-    n_obs, n_cell, loc,
-    heads_ref, well_ref, count_ref, obs_ref, std_ref, loc_ref, taper_ref, log_k_ref,
+    n_obs, n_cell,
+    heads_in, well_in, count_in, obs_in, std_in, loc_in, taper_in, log_k_ref,
     gram_ref, cov_ref,
-    field, send_heads, recv_heads, send_idx, recv_idx, obs_send, obs_all, pred_send, pred_all,
+    heads_ref, well_ref, count_ref, std_ref, loc_ref, taper_ref, in_sem, field, send_heads, recv_heads, send_idx, recv_idx, obs_send, obs_all, pred_send, pred_all,
     s_all, d_all, part, bands, band_sum, summed, field_sem, send_sem, recv_sem,
 ):
     total = n_obs * n_cell
     o, c = lax.axis_index("obs"), lax.axis_index("cell")
     me = o * n_cell + c
     cells, members = field.shape
-    wells = obs_ref.shape[0]
+    wells = obs_in.shape[0]
     slots = heads_ref.shape[0]
     piece_rows = cells // PIECES
 
@@ -57,6 +78,16 @@
         rows = pl.ds(p * piece_rows, piece_rows)
         return pltpu.make_async_copy(log_k_ref.at[rows], field.at[rows], field_sem.at[p])
 
+    inputs = [
+        pltpu.make_async_copy(src, dst, in_sem.at[i])
+        for i, (src, dst) in enumerate((
+            (well_in, well_ref), (count_in, count_ref), (heads_in, heads_ref),
+            (std_in, std_ref), (loc_in, loc_ref), (taper_in, taper_ref),
+            (obs_in, obs_send.at[pl.ds(0, wells)]),
+        ))
+    ]
+    for copy in inputs:
+        copy.start()
     for p in range(PIECES):
         piece_copy(p).start()
 
@@ -68,6 +99,9 @@
         pl.semaphore_signal(
             barrier, inc=1, device_id=(to // n_cell, lax.rem(to, n_cell)), device_id_type=MESH
         )
+
+    for copy in inputs:
+        copy.wait()
 
     well = well_ref[...]
     lane = lax.broadcasted_iota(jnp.int32, (1, slots), 1)
@@ -96,7 +130,6 @@
                 jnp.sum(ranks[q * CAP : (q + 1) * CAP], axis=0, keepdims=True) - 1.0
             )
 
-    obs_send[:wells, :] = obs_ref[...]
     obs_send[wells:, :] = jnp.broadcast_to(std_ref[...], (8, wells))
     pl.semaphore_wait(barrier, total - 1)
 
@@ -136,8 +169,15 @@
 
     to_cells(obs_send, obs_all, 2)
 
-    ones = jnp.ones((members, members), BF16)
-    step_rows = rows_per_step(piece_rows, 1024)
+    wide = (2 * members, 2 * members)
+    at_row = lax.broadcasted_iota(jnp.int32, wide, 0)
+    at_column = lax.broadcasted_iota(jnp.int32, wide, 1)
+    centring = jnp.where(at_row == at_column, 1.0, 0.0) - jnp.where(
+        (at_row < members) == (at_column < members), 1.0 / members, 0.0
+    )
+    centring = centring.astype(BF16)
+    step_rows = rows_per_step(piece_rows, 2048)
+    half_rows = step_rows // 2
     cov_ref[...] = jnp.zeros_like(cov_ref)
 
     def covariance(p):
@@ -146,10 +186,13 @@
         @pl.loop(0, piece_rows // step_rows)
         def _(i):
             at = pl.multiple_of(p * piece_rows + i * step_rows, step_rows)
-            x = field[pl.ds(at, step_rows), :]
-            mean = dot(x, ones) * (1.0 / members)
-            anomalies = (x.astype(F32) - mean).astype(BF16)
-            cov_ref[...] += dot_rows(anomalies, anomalies)
+            x = jnp.concatenate(
+                [field[pl.ds(at, half_rows), :], field[pl.ds(at + half_rows, half_rows), :]],
+                axis=1,
+            )
+            anomalies = dot(x, centring).astype(BF16)
+            left, right = anomalies[:, :members], anomalies[:, members:]
+            cov_ref[...] += dot_rows(left, left) + dot_rows(right, right)
 
     def arrived(ref, at):
         pltpu.make_async_copy(ref, ref, recv_sem.at[at]).wait()
@@ -163,7 +206,6 @@
     to_cells(pred_send, pred_all, 3)
 
     covariance(1)
-    covariance(2)
     arrived(obs_all, 2)
     arrived(pred_all, 3)
     eye = (
@@ -174,9 +216,10 @@
     @pl.loop(0, n_cell)
     def _(b):
         block = o * n_cell + b
-        weight = jnp.float32(0.0)
-        for k in range(loc):
-            weight = weight + jnp.where(loc_ref[c, k] == block, taper_ref[c, k], 0.0)
+        weight = jnp.sum(
+            jnp.where(loc_ref[pl.ds(c, 1), :] == block, taper_ref[pl.ds(c, 1), :], 0.0),
+            axis=1, keepdims=True,
+        )
         std = jnp.sum(
             jnp.where(eye, obs_all[b, pl.ds(wells, 1), :], 0.0), axis=1, keepdims=True
         )
@@ -205,6 +248,7 @@
         pltpu.make_async_copy(src_of(o), dst.at[o], recv_sem.at[at]).start()
 
     obs_copies(lambda to: part.at[to], bands, 4)
+    covariance(2)
     arrived(bands, 4)
     band_sum[...] = jnp.sum(bands[...], axis=0)
     obs_copies(lambda to: band_sum, summed, 5)
@@ -242,7 +286,10 @@
         group_copy(g, False).start()
 
     curvature = gram_ref[:, :members]
-    top = jnp.max(jnp.sum(jnp.abs(curvature), axis=1, keepdims=True))
+    square = product(curvature, curvature)
+    top = jnp.sqrt(jnp.max(jnp.sum(jnp.abs(square), axis=1, keepdims=True)))
+    top = jnp.minimum(top, jnp.max(jnp.sum(jnp.abs(curvature), axis=1, keepdims=True)))
+    cube = product(square, curvature)
     eye = jnp.where(
         lax.broadcasted_iota(jnp.int32, (members, members), 0)
         == lax.broadcasted_iota(jnp.int32, (members, members), 1),
@@ -250,16 +297,29 @@
     )
     shifts = [(1.0 + lambda_ref[l]) * (members - 1) for l in range(lambda_total)]
 
-    def system(l):
-        return gram_ref[:, :members] + shifts[l] * eye
+    def advance(rho):
+        return 2.0 / (2.0 - rho * rho), rho * rho / (2.0 - rho * rho)
+
+    def block(l):
+        return pl.ds(l * members, members)
 
     rhos = []
     for l in range(lambda_total):
-        first = 2.0 / (2.0 * shifts[l] + top)
-        rho = top * (0.5 * first)
-        gain = 2.0 / (2.0 - rho * rho)
-        inverse[l] = (gain * first) * (2.0 * eye - first * system(l))
-        rhos.append(rho * rho / (2.0 - rho * rho))
+        shift = shifts[l]
+        first = 2.0 / (2.0 * shift + top)
+        gain, rho = advance(top * (0.5 * first))
+        u, v = 2.0 * gain * first, gain * first * first
+        gain, rho = advance(rho)
+        terms = (
+            2.0 * u - 2.0 * v * shift - shift * (u - v * shift) * (u - v * shift),
+            -2.0 * v - (u - v * shift) * (u - 3.0 * v * shift),
+            v * (2.0 * u - 3.0 * v * shift),
+            -v * v,
+        )
+        inverse[block(l), :] = gain * (
+            terms[0] * eye + terms[1] * curvature + terms[2] * square + terms[3] * cube
+        )
+        rhos.append(rho)
 
     def largest(values):
         return functools.reduce(jnp.maximum, values)
@@ -267,34 +327,27 @@
     def step(carry):
         count, rhos = carry
         after = []
-        halves = [dot(system(l), inverse[l], HIGHEST) for l in range(lambda_total)]
+        shared = product(inverse[...], gram_ref[:, :members])
         for l in range(lambda_total):
-            rho = rhos[l]
-            gain = 2.0 / (2.0 - rho * rho)
-            x = inverse[l]
-            inverse[l] = gain * (2.0 * x - dot(x, halves[l], HIGHEST))
-            after.append(rho * rho / (2.0 - rho * rho))
+            gain, rho = advance(rhos[l])
+            x = inverse[block(l), :]
+            half = shared[l * members : (l + 1) * members] + shifts[l] * x
+            inverse[block(l), :] = gain * (2.0 * x - product(half, x))
+            after.append(rho)
         return count + 1, tuple(after)
 
     lax.while_loop(
-        lambda carry: (largest(carry[1]) > 2e-3) & (carry[0] < 40),
+        lambda carry: (largest(carry[1]) > 3e-5) & (carry[0] < 40),
         step,
         (jnp.int32(0), tuple(rhos)),
     )
 
-    right = gram_ref[:, members:]
-    firsts = [dot(inverse[l], right, HIGHEST) for l in range(lambda_total)]
-    misses = [right - dot(system(l), firsts[l], HIGHEST) for l in range(lambda_total)]
-    for l in range(lambda_total):
-        solved = firsts[l] + dot(inverse[l], misses[l], HIGHEST)
-        transform = solved.astype(BF16).astype(F32)
-        if l == 0:
-            centred = transform - jnp.mean(transform, axis=0, keepdims=True) + eye
-            high = centred.astype(BF16)
-            weights[:members, :] = high
-            weights[members:, :] = (centred - high.astype(F32)).astype(BF16)
-        spread = dot(cov_ref[...], transform, HIGHEST)
-        norms_ref[pl.ds(l, 1), :] = jnp.sum(transform * spread, axis=0, keepdims=True)
+    solved = product(inverse[...], gram_ref[:, members:]).astype(BF16)
+    transform = solved[:members].astype(F32)
+    centred = transform - jnp.mean(transform, axis=0, keepdims=True) + eye
+    high = centred.astype(BF16)
+    weights[:members, :] = high
+    weights[members:, :] = (centred - high.astype(F32)).astype(BF16)
 
     step_rows = rows_per_step(group_rows, 1024)
     for g in range(groups):
@@ -307,6 +360,17 @@
             field[rows, :] = dot(jnp.concatenate([x, x], axis=1), weights[...]).astype(BF16)
 
         group_copy(g, True).start()
+
+    beside = jnp.concatenate(
+        [solved[l * members : (l + 1) * members] for l in range(lambda_total)], axis=1
+    )
+    high, middle, low = split(cov_ref[...])
+    spread = dot(
+        jnp.concatenate([high, middle], axis=1), jnp.concatenate([beside, beside], axis=0)
+    ) + dot(low, beside)
+    norms = jnp.sum(beside.astype(F32) * spread, axis=0, keepdims=True)
+    for l in range(lambda_total):
+        norms_ref[pl.ds(l, 1), :] = norms[:, l * members : (l + 1) * members]
     for g in range(groups):
         group_copy(g, True).wait()
 
@@ -325,14 +389,21 @@
     smem = pl.BlockSpec(memory_space=pltpu.SMEM)
     hbm = pl.BlockSpec(memory_space=pl.ANY)
     gram, cov = pl.pallas_call(
-        functools.partial(gram_kernel, n_obs, n_cell, loc_blocks.shape[1]),
+        functools.partial(gram_kernel, n_obs, n_cell),
         out_shape=(
             jax.ShapeDtypeStruct((members, 2 * members), F32),
             jax.ShapeDtypeStruct((members, members), F32),
         ),
-        in_specs=[vmem, vmem, smem, vmem, vmem, smem, smem, hbm],
+        in_specs=[hbm] * 8,
         out_specs=(vmem, vmem),
         scratch_shapes=[
+            pltpu.VMEM((slots, members), BF16),
+            pltpu.VMEM((1, slots), jnp.int32),
+            pltpu.SMEM((1,), jnp.int32),
+            pltpu.VMEM((1, wells), F32),
+            pltpu.VMEM(loc_blocks.shape, jnp.int32),
+            pltpu.VMEM(taper.shape, F32),
+            pltpu.SemaphoreType.DMA((7,)),
             pltpu.VMEM((cells, members), BF16),
             pltpu.VMEM((total * CAP, members), BF16),
             pltpu.VMEM((total * CAP, members), BF16),
@@ -353,7 +424,7 @@
             pltpu.SemaphoreType.DMA((6,)),
         ],
         compiler_params=pltpu.CompilerParams(
-            collective_id=0, has_side_effects=True, vmem_limit_bytes=48 << 20
+            collective_id=0, has_side_effects=True, vmem_limit_bytes=60 << 20
         ),
         name="gram",
     )(
@@ -372,12 +443,12 @@
         out_specs=(hbm, vmem),
         scratch_shapes=[
             pltpu.VMEM((cells, members), BF16),
-            pltpu.VMEM((lambda_total, members, members), F32),
+            pltpu.VMEM((lambda_total * members, members), F32),
             pltpu.VMEM((2 * members, members), BF16),
             pltpu.SemaphoreType.DMA((groups,)),
             pltpu.SemaphoreType.DMA((groups,)),
         ],
-        compiler_params=pltpu.CompilerParams(vmem_limit_bytes=48 << 20),
+        compiler_params=pltpu.CompilerParams(vmem_limit_bytes=60 << 20),
         name="update",
     )(gram, cov, lambdas, log_k)
     return posterior, norms[None]

time: 68.4 us -> 62.6 us (0.915)
  local copies, waits for them, and re-layouts: 4.45 us -> 0 us
  Pallas kernels: 62.3 us -> 60.9 us
    unnamed x14 -> x0, local copies, waits for them, and re-layouts: 4.45 us -> none
    pallas_call x1, Pallas kernels: 21.5 us -> 19.9 us  [on_device(): pl.pallas_call(update_kernel, out_shape=(jax.ShapeDtypeStruct((cells, mem...]
where the time goes in v2:
time: 62.6 us; the launch traced here: 62.2 us
  Pallas kernels  60.9 us (97%)
  between operations  1.29 us (2%)
    pallas_call x1, Pallas kernels, on_device(): pl.pallas_call(functools.partial(gram_kernel, n_obs, n_cell), out_shape=(...  41 us
    pallas_call x1, Pallas kernels, on_device(): pl.pallas_call(update_kernel, out_shape=(jax.ShapeDtypeStruct((cells, mem...  19.9 us

profile of v2, /device:TPU:0, one launch (start us, length us, event | category | flops | bytes accessed | tf_op | source)
XLA Modules:
  0.0 62.2 jit_solution(6670693467161851527)
XLA Ops:
  1.3 41.0 %gram.1 = (f32[128,256]{1,0:T(8,128)}, f32[128,128]{1,0:T(8,128)}) custom-call(bf16[512,128]{1,0:T(8,128)(2,1)} %heads_in.1, s32[1,512]{1,0:T(1,128)} %bitcast.3, s32[1]{0:T(128)S(6)} %copy.11.count_in, f32[128,128]{1,0:T(8,128)} %obs_in.1, f32[1,128]{1,0:T(1,128)} %bitcast.4, s32[8,8]{1,0:T(8,128)} %loc_in.1, f32[8,8]{1,0:T(8,128)} %taper_in.1, ...), custom_call_target="tpu_custom_call" | custom-call | tf_op jit(solution)/shard_map/gram/pallas_call | solution.py:391
  42.3 19.9 %update.1 = (bf16[49152,128]{1,0:T(8,128)(2,1)}, f32[4,128]{1,0:T(4,128)}) custom-call(f32[128,256]{1,0:T(8,128)} %get-tuple-element.6.gram_ref, f32[128,128]{1,0:T(8,128)} %get-tuple-element.7.cov_ref, f32[4]{0:T(128)} %lambda_ref.1, bf16[49152,128]{1,0:T(8,128)(2,1)} %log_k_ref.3), custom_call_target="tpu_custom_call" | custom-call | tf_op jit(solution)/shard_map/update/pallas_call | solution.py:436

commit v3 on v2

--- a/solution.py
+++ b/solution.py
@@ -8,7 +8,7 @@
 from jax.sharding import PartitionSpec as P
 
 CAP = 16
-PIECES = 4
+PIECES = 6
 MESH = pl.DeviceIdType.MESH
 HIGHEST = lax.Precision.HIGHEST
 F32 = jnp.float32
@@ -63,12 +63,12 @@
     n_obs, n_cell,
     heads_in, well_in, count_in, obs_in, std_in, loc_in, taper_in, log_k_ref,
     gram_ref, cov_ref,
-    heads_ref, well_ref, count_ref, std_ref, loc_ref, taper_ref, in_sem, field, send_heads, recv_heads, send_idx, recv_idx, obs_send, obs_all, pred_send, pred_all,
-    s_all, d_all, part, bands, band_sum, summed, field_sem, send_sem, recv_sem,
+    heads_ref, well_ref, count_ref, std_ref, loc_ref, taper_ref, in_sem, field, squares,
+    send_heads, mid_heads, recv_heads, send_idx, mid_idx, recv_idx,
+    obs_send, obs_all, pred_send, pred_all, s_all, d_all, part, bands, band_sum, summed, field_sem, send_sem, recv_sem,
 ):
     total = n_obs * n_cell
     o, c = lax.axis_index("obs"), lax.axis_index("cell")
-    me = o * n_cell + c
     cells, members = field.shape
     wells = obs_in.shape[0]
     slots = heads_ref.shape[0]
@@ -93,11 +93,16 @@
 
     barrier = pltpu.get_barrier_semaphore()
 
-    @pl.loop(1, total)
+    @pl.loop(1, n_obs)
     def _(i):
-        to = lax.rem(me + i, total)
         pl.semaphore_signal(
-            barrier, inc=1, device_id=(to // n_cell, lax.rem(to, n_cell)), device_id_type=MESH
+            barrier, inc=1, device_id=(lax.rem(o + i, n_obs), c), device_id_type=MESH
+        )
+
+    @pl.loop(1, n_cell)
+    def _(i):
+        pl.semaphore_signal(
+            barrier, inc=1, device_id=(o, lax.rem(c + i, n_cell)), device_id_type=MESH
         )
 
     for copy in inputs:
@@ -131,43 +136,34 @@
             )
 
     obs_send[wells:, :] = jnp.broadcast_to(std_ref[...], (8, wells))
-    pl.semaphore_wait(barrier, total - 1)
-
-    def head_rows(d):
-        return pl.ds(pl.multiple_of(d * CAP, CAP), CAP)
-
-    @pl.loop(1, total)
-    def _(i):
-        to = lax.rem(me + i, total)
-        device = (to // n_cell, lax.rem(to, n_cell))
-        pltpu.make_async_remote_copy(
-            src_ref=send_heads.at[head_rows(to)], dst_ref=recv_heads.at[head_rows(me)],
-            send_sem=send_sem.at[0], recv_sem=recv_sem.at[0],
-            device_id=device, device_id_type=MESH,
-        ).start()
-        pltpu.make_async_remote_copy(
-            src_ref=send_idx.at[to], dst_ref=recv_idx.at[me],
-            send_sem=send_sem.at[1], recv_sem=recv_sem.at[1],
-            device_id=device, device_id_type=MESH,
-        ).start()
-
-    pltpu.make_async_copy(
-        send_heads.at[head_rows(me)], recv_heads.at[head_rows(me)], recv_sem.at[0]
-    ).start()
-    pltpu.make_async_copy(send_idx.at[me], recv_idx.at[me], recv_sem.at[1]).start()
-
-    def to_cells(src, dst, at):
+    pl.semaphore_wait(barrier, n_obs + n_cell - 2)
+
+    def to_obs(src_of, dst, at):
+        @pl.loop(1, n_obs)
+        def _(i):
+            to = lax.rem(o + i, n_obs)
+            pltpu.make_async_remote_copy(
+                src_ref=src_of(to), dst_ref=dst.at[o], send_sem=send_sem.at[at],
+                recv_sem=recv_sem.at[at], device_id=(to, c), device_id_type=MESH,
+            ).start()
+
+        pltpu.make_async_copy(src_of(o), dst.at[o], recv_sem.at[at]).start()
+
+    def to_cells(src_of, dst, at):
         @pl.loop(1, n_cell)
         def _(i):
+            to = lax.rem(c + i, n_cell)
             pltpu.make_async_remote_copy(
-                src_ref=src, dst_ref=dst.at[c], send_sem=send_sem.at[at],
-                recv_sem=recv_sem.at[at],
-                device_id=(o, lax.rem(c + i, n_cell)), device_id_type=MESH,
+                src_ref=src_of(to), dst_ref=dst.at[c], send_sem=send_sem.at[at],
+                recv_sem=recv_sem.at[at], device_id=(o, to), device_id_type=MESH,
             ).start()
 
-        pltpu.make_async_copy(src, dst.at[c], recv_sem.at[at]).start()
-
-    to_cells(obs_send, obs_all, 2)
+        pltpu.make_async_copy(src_of(c), dst.at[c], recv_sem.at[at]).start()
+
+    line = n_cell * CAP
+    to_obs(lambda to: send_heads.at[pl.ds(pl.multiple_of(to * line, line), line)], mid_heads, 0)
+    to_obs(lambda to: send_idx.at[pl.ds(to * n_cell, n_cell)], mid_idx, 1)
+    to_cells(lambda to: obs_send, obs_all, 2)
 
     wide = (2 * members, 2 * members)
     at_row = lax.broadcasted_iota(jnp.int32, wide, 0)
@@ -178,7 +174,7 @@
     centring = centring.astype(BF16)
     step_rows = rows_per_step(piece_rows, 2048)
     half_rows = step_rows // 2
-    cov_ref[...] = jnp.zeros_like(cov_ref)
+    squares[...] = jnp.zeros_like(squares)
 
     def covariance(p):
         piece_copy(p).wait()
@@ -191,21 +187,28 @@
                 axis=1,
             )
             anomalies = dot(x, centring).astype(BF16)
-            left, right = anomalies[:, :members], anomalies[:, members:]
-            cov_ref[...] += dot_rows(left, left) + dot_rows(right, right)
+            squares[...] += dot_rows(anomalies, anomalies)
 
     def arrived(ref, at):
         pltpu.make_async_copy(ref, ref, recv_sem.at[at]).wait()
 
     covariance(0)
-    arrived(recv_heads, 0)
-    arrived(recv_idx, 1)
+    arrived(mid_heads, 0)
+    arrived(mid_idx, 1)
+    to_cells(lambda to: mid_heads.at[:, pl.ds(pl.multiple_of(to * CAP, CAP), CAP)], recv_heads, 6)
+    to_cells(lambda to: mid_idx.at[:, to], recv_idx, 7)
+    covariance(1)
+    arrived(recv_heads, 6)
+    arrived(recv_idx, 7)
     ranks_at = lax.broadcasted_iota(jnp.int32, (total, CAP, wells), 1).astype(F32)
-    take = jnp.where(recv_idx[...] == ranks_at, 1.0, 0.0).reshape(total * CAP, wells)
-    pred_send[...] = dot_rows(take.astype(BF16), recv_heads[...]).astype(BF16)
-    to_cells(pred_send, pred_all, 3)
-
-    covariance(1)
+    ranks = recv_idx[...].reshape(total, 1, wells)
+    take = jnp.where(ranks == ranks_at, 1.0, 0.0).reshape(total * CAP, wells)
+    heads = recv_heads[...].reshape(total * CAP, members)
+    pred_send[...] = dot_rows(take.astype(BF16), heads).astype(BF16)
+    to_cells(lambda to: pred_send, pred_all, 3)
+
+    covariance(2)
+    covariance(3)
     arrived(obs_all, 2)
     arrived(pred_all, 3)
     eye = (
@@ -236,31 +239,23 @@
     band = members // n_obs
     part[...] = product.reshape(part.shape)
 
-    def obs_copies(src_of, dst, at):
-        @pl.loop(1, n_obs)
-        def _(i):
-            to = lax.rem(o + i, n_obs)
-            pltpu.make_async_remote_copy(
-                src_ref=src_of(to), dst_ref=dst.at[o], send_sem=send_sem.at[at],
-                recv_sem=recv_sem.at[at], device_id=(to, c), device_id_type=MESH,
-            ).start()
-
-        pltpu.make_async_copy(src_of(o), dst.at[o], recv_sem.at[at]).start()
-
-    obs_copies(lambda to: part.at[to], bands, 4)
-    covariance(2)
+    to_obs(lambda to: part.at[to], bands, 4)
+    covariance(4)
     arrived(bands, 4)
     band_sum[...] = jnp.sum(bands[...], axis=0)
-    obs_copies(lambda to: band_sum, summed, 5)
-    covariance(3)
+    to_obs(lambda to: band_sum, summed, 5)
+    covariance(5)
     arrived(summed, 5)
     gram_ref[...] = summed[...].reshape(gram_ref.shape)
+    cov_ref[...] = squares[:members, :members] + squares[members:, members:]
 
     def sent(ref, at):
         pltpu.make_async_copy(ref, ref, send_sem.at[at]).wait()
 
-    sent(recv_heads.at[pl.ds(0, (total - 1) * CAP)], 0)
-    sent(recv_idx.at[pl.ds(0, total - 1)], 1)
+    sent(mid_heads.at[pl.ds(0, n_obs - 1)], 0)
+    sent(mid_idx.at[pl.ds(0, n_obs - 1)], 1)
+    sent(recv_heads.at[pl.ds(0, n_cell - 1)], 6)
+    sent(recv_idx.at[pl.ds(0, n_cell - 1)], 7)
     sent(obs_all.at[pl.ds(0, n_cell - 1)], 2)
     sent(pred_all.at[pl.ds(0, n_cell - 1)], 3)
     sent(bands.at[pl.ds(0, n_obs - 1)], 4)
@@ -346,18 +341,25 @@
     transform = solved[:members].astype(F32)
     centred = transform - jnp.mean(transform, axis=0, keepdims=True) + eye
     high = centred.astype(BF16)
-    weights[:members, :] = high
-    weights[members:, :] = (centred - high.astype(F32)).astype(BF16)
-
-    step_rows = rows_per_step(group_rows, 1024)
+    low = (centred - high.astype(F32)).astype(BF16)
+    none = jnp.zeros_like(high)
+    weights[:members, :] = jnp.concatenate([high, none, low, none], axis=1)
+    weights[members:, :] = jnp.concatenate([none, high, none, low], axis=1)
+
+    step_rows = rows_per_step(group_rows, 2048)
+    half_rows = step_rows // 2
     for g in range(groups):
         group_copy(g, False).wait()
 
         @pl.loop(0, group_rows // step_rows)
         def _(i):
-            rows = pl.ds(pl.multiple_of(g * group_rows + i * step_rows, step_rows), step_rows)
-            x = field[rows, :]
-            field[rows, :] = dot(jnp.concatenate([x, x], axis=1), weights[...]).astype(BF16)
+            at = pl.multiple_of(g * group_rows + i * step_rows, step_rows)
+            upper, lower = pl.ds(at, half_rows), pl.ds(at + half_rows, half_rows)
+            x = jnp.concatenate([field[upper, :], field[lower, :]], axis=1)
+            both = dot(x, weights[...])
+            both = (both[:, : 2 * members] + both[:, 2 * members :]).astype(BF16)
+            field[upper, :] = both[:, :members]
+            field[lower, :] = both[:, members:]
 
         group_copy(g, True).start()
 
@@ -405,10 +407,13 @@
             pltpu.VMEM(taper.shape, F32),
             pltpu.SemaphoreType.DMA((7,)),
             pltpu.VMEM((cells, members), BF16),
+            pltpu.VMEM((2 * members, 2 * members), F32),
             pltpu.VMEM((total * CAP, members), BF16),
-            pltpu.VMEM((total * CAP, members), BF16),
+            pltpu.VMEM((n_obs, n_cell * CAP, members), BF16),
+            pltpu.VMEM((n_cell, n_obs, CAP, members), BF16),
             pltpu.VMEM((total, 1, wells), F32),
-            pltpu.VMEM((total, 1, wells), F32),
+            pltpu.VMEM((n_obs, n_cell, 1, wells), F32),
+            pltpu.VMEM((n_cell, n_obs, 1, wells), F32),
             pltpu.VMEM((wells + 8, members), F32),
             pltpu.VMEM((n_cell, wells + 8, members), F32),
             pltpu.VMEM((wells, members), BF16),
@@ -420,8 +425,8 @@
             pltpu.VMEM((band, 2 * members), F32),
             pltpu.VMEM((n_obs, band, 2 * members), F32),
             pltpu.SemaphoreType.DMA((PIECES,)),
-            pltpu.SemaphoreType.DMA((6,)),
-            pltpu.SemaphoreType.DMA((6,)),
+            pltpu.SemaphoreType.DMA((8,)),
+            pltpu.SemaphoreType.DMA((8,)),
         ],
         compiler_params=pltpu.CompilerParams(
             collective_id=0, has_side_effects=True, vmem_limit_bytes=60 << 20
@@ -444,7 +449,7 @@
         scratch_shapes=[
             pltpu.VMEM((cells, members), BF16),
             pltpu.VMEM((lambda_total * members, members), F32),
-            pltpu.VMEM((2 * members, members), BF16),
+            pltpu.VMEM((2 * members, 4 * members), BF16),
             pltpu.SemaphoreType.DMA((groups,)),
             pltpu.SemaphoreType.DMA((groups,)),
         ],

time: 62.6 us -> 59.4 us (0.949)
  Pallas kernels: 60.9 us -> 57.9 us
    pallas_call x1, Pallas kernels: 19.9 us -> 16.5 us  [on_device(): pl.pallas_call(update_kernel, out_shape=(jax.ShapeDtypeStruct((cells, mem...]
where the time goes in v3:
time: 59.4 us; the launch traced here: 59.2 us
  Pallas kernels  57.9 us (97%)
  between operations  1.29 us (2%)
    pallas_call x1, Pallas kernels, on_device(): pl.pallas_call(functools.partial(gram_kernel, n_obs, n_cell), out_shape=(...  41.5 us
    pallas_call x1, Pallas kernels, on_device(): pl.pallas_call(update_kernel, out_shape=(jax.ShapeDtypeStruct((cells, mem...  16.5 us

profile of v3, /device:TPU:0, one launch (start us, length us, event | category | flops | bytes accessed | tf_op | source)
XLA Modules:
  0.0 59.2 jit_solution(11447050724703453339)
XLA Ops:
  1.3 41.5 %gram.1 = (f32[128,256]{1,0:T(8,128)}, f32[128,128]{1,0:T(8,128)}) custom-call(bf16[512,128]{1,0:T(8,128)(2,1)} %heads_in.1, s32[1,512]{1,0:T(1,128)} %bitcast.3, s32[1]{0:T(128)S(6)} %copy.11.count_in, f32[128,128]{1,0:T(8,128)} %obs_in.1, f32[1,128]{1,0:T(1,128)} %bitcast.4, s32[8,8]{1,0:T(8,128)} %loc_in.1, f32[8,8]{1,0:T(8,128)} %taper_in.1, ...), custom_call_target="tpu_custom_call" | custom-call | tf_op jit(solution)/shard_map/gram/pallas_call | solution.py:393
  42.7 16.5 %update.1 = (bf16[49152,128]{1,0:T(8,128)(2,1)}, f32[4,128]{1,0:T(4,128)}) custom-call(f32[128,256]{1,0:T(8,128)} %get-tuple-element.6.gram_ref, f32[128,128]{1,0:T(8,128)} %get-tuple-element.7.cov_ref, f32[4]{0:T(128)} %lambda_ref.1, bf16[49152,128]{1,0:T(8,128)(2,1)} %log_k_ref.3), custom_call_target="tpu_custom_call" | custom-call | tf_op jit(solution)/shard_map/update/pallas_call | solution.py:441

commit v4 on v3

--- a/solution.py
+++ b/solution.py
@@ -165,15 +165,12 @@
     to_obs(lambda to: send_idx.at[pl.ds(to * n_cell, n_cell)], mid_idx, 1)
     to_cells(lambda to: obs_send, obs_all, 2)
 
-    wide = (2 * members, 2 * members)
-    at_row = lax.broadcasted_iota(jnp.int32, wide, 0)
-    at_column = lax.broadcasted_iota(jnp.int32, wide, 1)
-    centring = jnp.where(at_row == at_column, 1.0, 0.0) - jnp.where(
-        (at_row < members) == (at_column < members), 1.0 / members, 0.0
-    )
-    centring = centring.astype(BF16)
-    step_rows = rows_per_step(piece_rows, 2048)
-    half_rows = step_rows // 2
+    square = (members, members)
+    centring = jnp.where(
+        lax.broadcasted_iota(jnp.int32, square, 0) == lax.broadcasted_iota(jnp.int32, square, 1),
+        1.0 - 1.0 / members, -1.0 / members,
+    ).astype(BF16)
+    step_rows = rows_per_step(piece_rows, 1024)
     squares[...] = jnp.zeros_like(squares)
 
     def covariance(p):
@@ -182,12 +179,11 @@
         @pl.loop(0, piece_rows // step_rows)
         def _(i):
             at = pl.multiple_of(p * piece_rows + i * step_rows, step_rows)
-            x = jnp.concatenate(
-                [field[pl.ds(at, half_rows), :], field[pl.ds(at + half_rows, half_rows), :]],
-                axis=1,
+            x = field[pl.ds(at, step_rows), :]
+            anomalies = lax.dot_general(
+                centring, x, (((1,), (1,)), ((), ())), preferred_element_type=F32
             )
-            anomalies = dot(x, centring).astype(BF16)
-            squares[...] += dot_rows(anomalies, anomalies)
+            squares[...] += dot(anomalies.astype(BF16), x)
 
     def arrived(ref, at):
         pltpu.make_async_copy(ref, ref, recv_sem.at[at]).wait()
@@ -247,7 +243,7 @@
     covariance(5)
     arrived(summed, 5)
     gram_ref[...] = summed[...].reshape(gram_ref.shape)
-    cov_ref[...] = squares[:members, :members] + squares[members:, members:]
+    cov_ref[...] = squares[...] - jnp.mean(squares[...], axis=1, keepdims=True)
 
     def sent(ref, at):
         pltpu.make_async_copy(ref, ref, send_sem.at[at]).wait()
@@ -341,10 +337,8 @@
     transform = solved[:members].astype(F32)
     centred = transform - jnp.mean(transform, axis=0, keepdims=True) + eye
     high = centred.astype(BF16)
-    low = (centred - high.astype(F32)).astype(BF16)
-    none = jnp.zeros_like(high)
-    weights[:members, :] = jnp.concatenate([high, none, low, none], axis=1)
-    weights[members:, :] = jnp.concatenate([none, high, none, low], axis=1)
+    weights[:members, :] = high
+    weights[members:, :] = (centred - high.astype(F32)).astype(BF16)
 
     step_rows = rows_per_step(group_rows, 2048)
     half_rows = step_rows // 2
@@ -355,11 +349,9 @@
         def _(i):
             at = pl.multiple_of(g * group_rows + i * step_rows, step_rows)
             upper, lower = pl.ds(at, half_rows), pl.ds(at + half_rows, half_rows)
-            x = jnp.concatenate([field[upper, :], field[lower, :]], axis=1)
-            both = dot(x, weights[...])
-            both = (both[:, : 2 * members] + both[:, 2 * members :]).astype(BF16)
-            field[upper, :] = both[:, :members]
-            field[lower, :] = both[:, members:]
+            for rows in (upper, lower):
+                x = field[rows, :]
+                field[rows, :] = dot(jnp.concatenate([x, x], axis=1), weights[...]).astype(BF16)
 
         group_copy(g, True).start()
 
@@ -407,7 +399,7 @@
             pltpu.VMEM(taper.shape, F32),
             pltpu.SemaphoreType.DMA((7,)),
             pltpu.VMEM((cells, members), BF16),
-            pltpu.VMEM((2 * members, 2 * members), F32),
+            pltpu.VMEM((members, members), F32),
             pltpu.VMEM((total * CAP, members), BF16),
             pltpu.VMEM((n_obs, n_cell * CAP, members), BF16),
             pltpu.VMEM((n_cell, n_obs, CAP, members), BF16),
@@ -449,7 +441,7 @@
         scratch_shapes=[
             pltpu.VMEM((cells, members), BF16),
             pltpu.VMEM((lambda_total * members, members), F32),
-            pltpu.VMEM((2 * members, 4 * members), BF16),
+            pltpu.VMEM((2 * members, members), BF16),
             pltpu.SemaphoreType.DMA((groups,)),
             pltpu.SemaphoreType.DMA((groups,)),
         ],

time: 59.4 us -> 68.4 us (1.15)
  Pallas kernels: 57.9 us -> 67.2 us
    pallas_call x1, Pallas kernels: 16.5 us -> 25.5 us  [on_device(): pl.pallas_call(update_kernel, out_shape=(jax.ShapeDtypeStruct((cells, mem...]
where the time goes in v4:
time: 68.4 us
  Pallas kernels  67.2 us (98%)
  between operations  1.29 us (2%)
    pallas_call x1, Pallas kernels, on_device(): pl.pallas_call(functools.partial(gram_kernel, n_obs, n_cell), out_shape=(...  41.6 us
    pallas_call x1, Pallas kernels, on_device(): pl.pallas_call(update_kernel, out_shape=(jax.ShapeDtypeStruct((cells, mem...  25.5 us

profile of v4, /device:TPU:0, one launch (start us, length us, event | category | flops | bytes accessed | tf_op | source)
XLA Modules:
  0.0 68.4 jit_solution(13190881455936219880)
XLA Ops:
  1.3 41.6 %gram.1 = (f32[128,256]{1,0:T(8,128)}, f32[128,128]{1,0:T(8,128)}) custom-call(bf16[512,128]{1,0:T(8,128)(2,1)} %heads_in.1, s32[1,512]{1,0:T(1,128)} %bitcast.3, s32[1]{0:T(128)S(6)} %copy.11.count_in, f32[128,128]{1,0:T(8,128)} %obs_in.1, f32[1,128]{1,0:T(1,128)} %bitcast.4, s32[8,8]{1,0:T(8,128)} %loc_in.1, f32[8,8]{1,0:T(8,128)} %taper_in.1, ...), custom_call_target="tpu_custom_call" | custom-call | tf_op jit(solution)/shard_map/gram/pallas_call | solution.py:385
  42.9 25.5 %update.1 = (bf16[49152,128]{1,0:T(8,128)(2,1)}, f32[4,128]{1,0:T(4,128)}) custom-call(f32[128,256]{1,0:T(8,128)} %get-tuple-element.6.gram_ref, f32[128,128]{1,0:T(8,128)} %get-tuple-element.7.cov_ref, f32[4]{0:T(128)} %lambda_ref.1, bf16[49152,128]{1,0:T(8,128)(2,1)} %log_k_ref.3), custom_call_target="tpu_custom_call" | custom-call | tf_op jit(solution)/shard_map/update/pallas_call | solution.py:433

commit v5 on v4

--- a/solution.py
+++ b/solution.py
@@ -65,7 +65,7 @@
     gram_ref, cov_ref,
     heads_ref, well_ref, count_ref, std_ref, loc_ref, taper_ref, in_sem, field, squares,
     send_heads, mid_heads, recv_heads, send_idx, mid_idx, recv_idx,
-    obs_send, obs_all, pred_send, pred_all, s_all, d_all, part, bands, band_sum, summed, field_sem, send_sem, recv_sem,
+    obs_ref, part, terms, got, bands, band_sum, summed, field_sem, send_sem, recv_sem,
 ):
     total = n_obs * n_cell
     o, c = lax.axis_index("obs"), lax.axis_index("cell")
@@ -83,7 +83,7 @@
         for i, (src, dst) in enumerate((
             (well_in, well_ref), (count_in, count_ref), (heads_in, heads_ref),
             (std_in, std_ref), (loc_in, loc_ref), (taper_in, taper_ref),
-            (obs_in, obs_send.at[pl.ds(0, wells)]),
+            (obs_in, obs_ref),
         ))
     ]
     for copy in inputs:
@@ -135,7 +135,6 @@
                 jnp.sum(ranks[q * CAP : (q + 1) * CAP], axis=0, keepdims=True) - 1.0
             )
 
-    obs_send[wells:, :] = jnp.broadcast_to(std_ref[...], (8, wells))
     pl.semaphore_wait(barrier, n_obs + n_cell - 2)
 
     def to_obs(src_of, dst, at):
@@ -163,7 +162,6 @@
     line = n_cell * CAP
     to_obs(lambda to: send_heads.at[pl.ds(pl.multiple_of(to * line, line), line)], mid_heads, 0)
     to_obs(lambda to: send_idx.at[pl.ds(to * n_cell, n_cell)], mid_idx, 1)
-    to_cells(lambda to: obs_send, obs_all, 2)
 
     square = (members, members)
     centring = jnp.where(
@@ -188,57 +186,46 @@
     def arrived(ref, at):
         pltpu.make_async_copy(ref, ref, recv_sem.at[at]).wait()
 
+    eye = (
+        lax.broadcasted_iota(jnp.int32, (wells, wells), 0)
+        == lax.broadcasted_iota(jnp.int32, (wells, wells), 1)
+    )
+    inverse = 1.0 / jnp.sum(jnp.where(eye, std_ref[...], 0.0), axis=1, keepdims=True)
+    tile_weights = [
+        jnp.sum(
+            jnp.where(loc_ref[...] == b * n_cell + c, taper_ref[...], 0.0),
+            axis=1, keepdims=True,
+        )
+        for b in range(n_obs)
+    ]
+
     covariance(0)
     arrived(mid_heads, 0)
     arrived(mid_idx, 1)
-    to_cells(lambda to: mid_heads.at[:, pl.ds(pl.multiple_of(to * CAP, CAP), CAP)], recv_heads, 6)
-    to_cells(lambda to: mid_idx.at[:, to], recv_idx, 7)
+    to_cells(lambda to: mid_heads.at[:, pl.ds(pl.multiple_of(to * CAP, CAP), CAP)], recv_heads, 2)
+    to_cells(lambda to: mid_idx.at[:, to], recv_idx, 6)
     covariance(1)
-    arrived(recv_heads, 6)
-    arrived(recv_idx, 7)
+    arrived(recv_heads, 2)
+    arrived(recv_idx, 6)
     ranks_at = lax.broadcasted_iota(jnp.int32, (total, CAP, wells), 1).astype(F32)
     ranks = recv_idx[...].reshape(total, 1, wells)
     take = jnp.where(ranks == ranks_at, 1.0, 0.0).reshape(total * CAP, wells)
     heads = recv_heads[...].reshape(total * CAP, members)
-    pred_send[...] = dot_rows(take.astype(BF16), heads).astype(BF16)
-    to_cells(lambda to: pred_send, pred_all, 3)
-
+    pred = dot_rows(take.astype(BF16), heads)
+    scaled = (pred - jnp.mean(pred, axis=1, keepdims=True)) * inverse
+    innovation = (obs_ref[...] - pred) * inverse
+    joined = jnp.concatenate([scaled, innovation], axis=1)
+    part[...] = dot_rows(scaled, joined, HIGHEST).reshape(part.shape)
+    to_obs(lambda to: part.at[to], bands, 4)
     covariance(2)
+    arrived(bands, 4)
+    for t in range(n_cell):
+        terms[t] = sum(tile_weights[b][t : t + 1, :] * bands[b] for b in range(n_obs))
+    to_cells(lambda to: terms.at[to], got, 3)
     covariance(3)
-    arrived(obs_all, 2)
-    arrived(pred_all, 3)
-    eye = (
-        lax.broadcasted_iota(jnp.int32, (wells, wells), 0)
-        == lax.broadcasted_iota(jnp.int32, (wells, wells), 1)
-    )
-
-    @pl.loop(0, n_cell)
-    def _(b):
-        block = o * n_cell + b
-        weight = jnp.sum(
-            jnp.where(loc_ref[pl.ds(c, 1), :] == block, taper_ref[pl.ds(c, 1), :], 0.0),
-            axis=1, keepdims=True,
-        )
-        std = jnp.sum(
-            jnp.where(eye, obs_all[b, pl.ds(wells, 1), :], 0.0), axis=1, keepdims=True
-        )
-        inverse = 1.0 / std
-        pred = pred_all[b].astype(F32)
-        mean = jnp.mean(pred, axis=1, keepdims=True)
-        scaled = (pred - mean) * inverse
-        rows = pl.ds(pl.multiple_of(b * wells, wells), wells)
-        s_all[rows, :] = scaled * weight
-        d_all[rows, :members] = scaled
-        d_all[rows, members:] = (obs_all[b, pl.ds(0, wells), :] - pred) * inverse
-
-    product = dot_rows(s_all[...], d_all[...], HIGHEST)
-    band = members // n_obs
-    part[...] = product.reshape(part.shape)
-
-    to_obs(lambda to: part.at[to], bands, 4)
     covariance(4)
-    arrived(bands, 4)
-    band_sum[...] = jnp.sum(bands[...], axis=0)
+    arrived(got, 3)
+    band_sum[...] = jnp.sum(got[...], axis=0)
     to_obs(lambda to: band_sum, summed, 5)
     covariance(5)
     arrived(summed, 5)
@@ -250,10 +237,9 @@
 
     sent(mid_heads.at[pl.ds(0, n_obs - 1)], 0)
     sent(mid_idx.at[pl.ds(0, n_obs - 1)], 1)
-    sent(recv_heads.at[pl.ds(0, n_cell - 1)], 6)
-    sent(recv_idx.at[pl.ds(0, n_cell - 1)], 7)
-    sent(obs_all.at[pl.ds(0, n_cell - 1)], 2)
-    sent(pred_all.at[pl.ds(0, n_cell - 1)], 3)
+    sent(recv_heads.at[pl.ds(0, n_cell - 1)], 2)
+    sent(recv_idx.at[pl.ds(0, n_cell - 1)], 6)
+    sent(got.at[pl.ds(0, n_cell - 1)], 3)
     sent(bands.at[pl.ds(0, n_obs - 1)], 4)
     sent(summed.at[pl.ds(0, n_obs - 1)], 5)
 
@@ -337,10 +323,12 @@
     transform = solved[:members].astype(F32)
     centred = transform - jnp.mean(transform, axis=0, keepdims=True) + eye
     high = centred.astype(BF16)
-    weights[:members, :] = high
-    weights[members:, :] = (centred - high.astype(F32)).astype(BF16)
-
-    step_rows = rows_per_step(group_rows, 2048)
+    low = (centred - high.astype(F32)).astype(BF16)
+    none = jnp.zeros_like(high)
+    weights[:members, :] = jnp.concatenate([high, none, low, none], axis=1)
+    weights[members:, :] = jnp.concatenate([none, high, none, low], axis=1)
+
+    step_rows = rows_per_step(group_rows, 1024)
     half_rows = step_rows // 2
     for g in range(groups):
         group_copy(g, False).wait()
@@ -349,9 +337,11 @@
         def _(i):
             at = pl.multiple_of(g * group_rows + i * step_rows, step_rows)
             upper, lower = pl.ds(at, half_rows), pl.ds(at + half_rows, half_rows)
-            for rows in (upper, lower):
-                x = field[rows, :]
-                field[rows, :] = dot(jnp.concatenate([x, x], axis=1), weights[...]).astype(BF16)
+            x = jnp.concatenate([field[upper, :], field[lower, :]], axis=1)
+            both = dot(x, weights[...])
+            both = (both[:, : 2 * members] + both[:, 2 * members :]).astype(BF16)
+            field[upper, :] = both[:, :members]
+            field[lower, :] = both[:, members:]
 
         group_copy(g, True).start()
 
@@ -406,19 +396,16 @@
             pltpu.VMEM((total, 1, wells), F32),
             pltpu.VMEM((n_obs, n_cell, 1, wells), F32),
             pltpu.VMEM((n_cell, n_obs, 1, wells), F32),
-            pltpu.VMEM((wells + 8, members), F32),
-            pltpu.VMEM((n_cell, wells + 8, members), F32),
-            pltpu.VMEM((wells, members), BF16),
-            pltpu.VMEM((n_cell, wells, members), BF16),
-            pltpu.VMEM((n_cell * wells, members), F32),
-            pltpu.VMEM((n_cell * wells, 2 * members), F32),
+            pltpu.VMEM((wells, members), F32),
             pltpu.VMEM((n_obs, band, 2 * members), F32),
+            pltpu.VMEM((n_cell, band, 2 * members), F32),
+            pltpu.VMEM((n_cell, band, 2 * members), F32),
             pltpu.VMEM((n_obs, band, 2 * members), F32),
             pltpu.VMEM((band, 2 * members), F32),
             pltpu.VMEM((n_obs, band, 2 * members), F32),
             pltpu.SemaphoreType.DMA((PIECES,)),
-            pltpu.SemaphoreType.DMA((8,)),
-            pltpu.SemaphoreType.DMA((8,)),
+            pltpu.SemaphoreType.DMA((7,)),
+            pltpu.SemaphoreType.DMA((7,)),
         ],
         compiler_params=pltpu.CompilerParams(
             collective_id=0, has_side_effects=True, vmem_limit_bytes=60 << 20
@@ -441,7 +428,7 @@
         scratch_shapes=[
             pltpu.VMEM((cells, members), BF16),
             pltpu.VMEM((lambda_total * members, members), F32),
-            pltpu.VMEM((2 * members, members), BF16),
+            pltpu.VMEM((2 * members, 4 * members), BF16),
             pltpu.SemaphoreType.DMA((groups,)),
             pltpu.SemaphoreType.DMA((groups,)),
         ],

time: 68.4 us -> 54.2 us (0.79)
  Pallas kernels: 67.2 us -> 52.8 us
    pallas_call x1, Pallas kernels: 41.6 us -> 32.4 us  [on_device(): pl.pallas_call(functools.partial(gram_kernel, n_obs, n_cell), out_shape=(...]
    pallas_call x1, Pallas kernels: 25.5 us -> 20.3 us  [on_device(): pl.pallas_call(update_kernel, out_shape=(jax.ShapeDtypeStruct((cells, mem...]
where the time goes in v5:
time: 54.2 us; the launch traced here: 54 us
  Pallas kernels  52.8 us (97%)
  between operations  1.29 us (2%)
    pallas_call x1, Pallas kernels, on_device(): pl.pallas_call(functools.partial(gram_kernel, n_obs, n_cell), out_shape=(...  32.4 us
    pallas_call x1, Pallas kernels, on_device(): pl.pallas_call(update_kernel, out_shape=(jax.ShapeDtypeStruct((cells, mem...  20.3 us

profile of v5, /device:TPU:0, one launch (start us, length us, event | category | flops | bytes accessed | tf_op | source)
XLA Modules:
  0.0 54.0 jit_solution(14937384397155313521)
XLA Ops:
  1.3 32.4 %gram.1 = (f32[128,256]{1,0:T(8,128)}, f32[128,128]{1,0:T(8,128)}) custom-call(bf16[512,128]{1,0:T(8,128)(2,1)} %heads_in.1, s32[1,512]{1,0:T(1,128)} %bitcast.3, s32[1]{0:T(128)S(6)} %copy.11.count_in, f32[128,128]{1,0:T(8,128)} %obs_in.1, f32[1,128]{1,0:T(1,128)} %bitcast.4, s32[8,8]{1,0:T(8,128)} %loc_in.1, f32[8,8]{1,0:T(8,128)} %taper_in.1, ...), custom_call_target="tpu_custom_call" | custom-call | tf_op jit(solution)/shard_map/gram/pallas_call | solution.py:375
  33.7 20.3 %update.1 = (bf16[49152,128]{1,0:T(8,128)(2,1)}, f32[4,128]{1,0:T(4,128)}) custom-call(f32[128,256]{1,0:T(8,128)} %get-tuple-element.6.gram_ref, f32[128,128]{1,0:T(8,128)} %get-tuple-element.7.cov_ref, f32[4]{0:T(128)} %lambda_ref.1, bf16[49152,128]{1,0:T(8,128)(2,1)} %log_k_ref.3), custom_call_target="tpu_custom_call" | custom-call | tf_op jit(solution)/shard_map/update/pallas_call | solution.py:420

commit v6 on v5

--- a/solution.py
+++ b/solution.py
@@ -168,7 +168,7 @@
         lax.broadcasted_iota(jnp.int32, square, 0) == lax.broadcasted_iota(jnp.int32, square, 1),
         1.0 - 1.0 / members, -1.0 / members,
     ).astype(BF16)
-    step_rows = rows_per_step(piece_rows, 1024)
+    step_rows = rows_per_step(piece_rows, 4096)
     squares[...] = jnp.zeros_like(squares)
 
     def covariance(p):
@@ -328,7 +328,7 @@
     weights[:members, :] = jnp.concatenate([high, none, low, none], axis=1)
     weights[members:, :] = jnp.concatenate([none, high, none, low], axis=1)
 
-    step_rows = rows_per_step(group_rows, 1024)
+    step_rows = rows_per_step(group_rows, 4096)
     half_rows = step_rows // 2
     for g in range(groups):
         group_copy(g, False).wait()

time: 54.2 us -> 54.2 us (level)
    pallas_call x1, Pallas kernels: 20.3 us -> 21.2 us  [on_device(): pl.pallas_call(update_kernel, out_shape=(jax.ShapeDtypeStruct((cells, mem...]
    pallas_call x1, Pallas kernels: 32.4 us -> 31.6 us  [on_device(): pl.pallas_call(functools.partial(gram_kernel, n_obs, n_cell), out_shape=(...]
where the time goes in v6:
time: 54.2 us
  Pallas kernels  52.8 us (97%)
  between operations  1.45 us (3%)
    pallas_call x1, Pallas kernels, on_device(): pl.pallas_call(functools.partial(gram_kernel, n_obs, n_cell), out_shape=(...  31.6 us
    pallas_call x1, Pallas kernels, on_device(): pl.pallas_call(update_kernel, out_shape=(jax.ShapeDtypeStruct((cells, mem...  21.2 us

profile of v6, /device:TPU:0, one launch (start us, length us, event | category | flops | bytes accessed | tf_op | source)
XLA Modules:
  0.0 54.2 jit_solution(1486592805092614176)
XLA Ops:
  1.3 31.6 %gram.1 = (f32[128,256]{1,0:T(8,128)}, f32[128,128]{1,0:T(8,128)}) custom-call(bf16[512,128]{1,0:T(8,128)(2,1)} %heads_in.1, s32[1,512]{1,0:T(1,128)} %bitcast.3, s32[1]{0:T(128)S(6)} %copy.11.count_in, f32[128,128]{1,0:T(8,128)} %obs_in.1, f32[1,128]{1,0:T(1,128)} %bitcast.4, s32[8,8]{1,0:T(8,128)} %loc_in.1, f32[8,8]{1,0:T(8,128)} %taper_in.1, ...), custom_call_target="tpu_custom_call" | custom-call | tf_op jit(solution)/shard_map/gram/pallas_call | solution.py:375
  32.9 21.2 %update.1 = (bf16[49152,128]{1,0:T(8,128)(2,1)}, f32[4,128]{1,0:T(4,128)}) custom-call(f32[128,256]{1,0:T(8,128)} %get-tuple-element.6.gram_ref, f32[128,128]{1,0:T(8,128)} %get-tuple-element.7.cov_ref, f32[4]{0:T(128)} %lambda_ref.1, bf16[49152,128]{1,0:T(8,128)(2,1)} %log_k_ref.3), custom_call_target="tpu_custom_call" | custom-call | tf_op jit(solution)/shard_map/update/pallas_call | solution.py:420

commit v7 on v6

--- a/solution.py
+++ b/solution.py
@@ -328,7 +328,7 @@
     weights[:members, :] = jnp.concatenate([high, none, low, none], axis=1)
     weights[members:, :] = jnp.concatenate([none, high, none, low], axis=1)
 
-    step_rows = rows_per_step(group_rows, 4096)
+    step_rows = rows_per_step(group_rows, 2048)
     half_rows = step_rows // 2
     for g in range(groups):
         group_copy(g, False).wait()

time: 54.2 us -> 49.5 us (0.913)
  Pallas kernels: 52.8 us -> 48.1 us
    pallas_call x1, Pallas kernels: 21.2 us -> 16.5 us  [on_device(): pl.pallas_call(update_kernel, out_shape=(jax.ShapeDtypeStruct((cells, mem...]
where the time goes in v7:
time: 49.5 us; the launch traced here: 49.3 us
  Pallas kernels  48.1 us (97%)
  between operations  1.29 us (3%)
    pallas_call x1, Pallas kernels, on_device(): pl.pallas_call(functools.partial(gram_kernel, n_obs, n_cell), out_shape=(...  31.6 us
    pallas_call x1, Pallas kernels, on_device(): pl.pallas_call(update_kernel, out_shape=(jax.ShapeDtypeStruct((cells, mem...  16.5 us

profile of v7, /device:TPU:0, one launch (start us, length us, event | category | flops | bytes accessed | tf_op | source)
XLA Modules:
  0.0 49.3 jit_solution(16243481916506924709)
XLA Ops:
  1.3 31.6 %gram.1 = (f32[128,256]{1,0:T(8,128)}, f32[128,128]{1,0:T(8,128)}) custom-call(bf16[512,128]{1,0:T(8,128)(2,1)} %heads_in.1, s32[1,512]{1,0:T(1,128)} %bitcast.3, s32[1]{0:T(128)S(6)} %copy.11.count_in, f32[128,128]{1,0:T(8,128)} %obs_in.1, f32[1,128]{1,0:T(1,128)} %bitcast.4, s32[8,8]{1,0:T(8,128)} %loc_in.1, f32[8,8]{1,0:T(8,128)} %taper_in.1, ...), custom_call_target="tpu_custom_call" | custom-call | tf_op jit(solution)/shard_map/gram/pallas_call | solution.py:375
  32.9 16.5 %update.1 = (bf16[49152,128]{1,0:T(8,128)(2,1)}, f32[4,128]{1,0:T(4,128)}) custom-call(f32[128,256]{1,0:T(8,128)} %get-tuple-element.6.gram_ref, f32[128,128]{1,0:T(8,128)} %get-tuple-element.7.cov_ref, f32[4]{0:T(128)} %lambda_ref.1, bf16[49152,128]{1,0:T(8,128)(2,1)} %log_k_ref.3), custom_call_target="tpu_custom_call" | custom-call | tf_op jit(solution)/shard_map/update/pallas_call | solution.py:420
